TPU v7x, 32 devices: a whole 2x2x4 slice. The times are simulated.
32 devices in a mesh: groups: 2 (over x), blk: 8 (over z, y), rows: 2 (over core).
Axes of the slice: x: 2, y: 2, z: 4, core: 2. Of those that a mesh axis runs over, the one named last changes fastest.
Arguments:
- queries: bfloat16 [256, 2048], P(('groups', 'blk'), 'rows'), parts along dimension 0, may hold values from -170 to 170
- cache_keys: bfloat16 [8192, 256], P(('groups', 'blk'), 'rows'), parts along dimension 0, may hold values from -6 to 6
- cache_values: bfloat16 [8192, 256], P(('groups', 'blk'), 'rows'), parts along dimension 0, may hold values from -6 to 6
- span_starts: int32 [4], P('groups'), parts along dimension 0, may hold values from 0 to 4032, as said below
- out_weight: bfloat16 [2048, 2048], P(('rows', 'blk')), may hold values from -0.125 to 0.125
- norm_gain: bfloat16 [2048], replicated, may hold values from 0.099609375 to 1.8984375
- expert_ids: int32 [256, 8], P(('groups', 'blk', 'rows')), parts along dimension 0, may hold values from 0 to 15, all different within a row; in each aligned block of 8 rows (0 to 7, 8 to 15, ...) at most 8 rows name the same one
- gate_fixed: int32 [256, 8], P(('groups', 'blk', 'rows')), parts along dimension 0, may hold values from 1 to 4095
- gate_weight: bfloat16 [16, 2048, 768], P(('blk', 'rows')), may hold values from -0.125 to 0.125
- up_weight: bfloat16 [16, 2048, 768], P(('blk', 'rows')), may hold values from -0.125 to 0.125
- down_weight: bfloat16 [16, 768, 2048], P(('blk', 'rows')), may hold values from -0.21875 to 0.21875
Outputs:
- attn_proj: bfloat16 [256, 2048], P(('groups', 'blk', 'rows')), parts along dimension 0
- expert_out: bfloat16 [256, 2048], P(('groups', 'blk', 'rows')), parts along dimension 0
There are 2 independent parts, one for each index of `groups`. A program takes and returns all parts, laid end to end along the dimension named above; an argument that names none is the same for every part. Nothing has to cross between parts.
Inputs may be any that keep to these rules, and one draw needn't show every extreme that they name: `span_starts`: the last span ends at the last cached position, entry 1 is 4032; entry 0 is at most 3968. `expert_ids`: each token names 8 different experts; among the tokens of one device (aligned blocks of 8 rows) no expert is named more than 8 times.
All inputs are finite; a program needn't handle non-finite values.
Results may differ from a plain program's by a relative error of at most 0.035.
Values may be sent and summed in bfloat16 or wider, within the bound.
A program may use at most 64 MiB of HBM per device.

v0:
```python
import math

import jax
import jax.numpy as jnp
from jax import lax
from jax.sharding import PartitionSpec as P

HD = 128
SPANS = 2


NEG_FILL = -1e30
EPSILON = 1e-06


def partial_attention(query_block, query_pos, cache_keys, cache_values, key_pos):
    rows_here = query_block.shape[0]
    kv_local = cache_keys.shape[1] // HD
    group_size = query_block.shape[1] // (kv_local * HD)
    heads_here = kv_local * group_size
    shaped_q = query_block.reshape(rows_here, kv_local, group_size, HD)
    shaped_k = cache_keys.reshape(-1, kv_local, HD)
    shaped_v = cache_values.reshape(-1, kv_local, HD)
    scores = jnp.einsum(
        "qgjd,kgd->qgjk", shaped_q, shaped_k, preferred_element_type=jnp.float32
    ) * (1.0 / math.sqrt(HD))
    visible = (key_pos[None, :] <= query_pos[:, None])[:, None, None, :]
    scores = jnp.where(visible, scores, NEG_FILL)
    row_top = jnp.max(scores, axis=-1)
    weights = jnp.where(visible, jnp.exp(scores - row_top[..., None]), 0.0)
    totals = jnp.sum(weights, axis=-1)
    numerator = jnp.einsum(
        "qgjk,kgd->qgjd", weights.astype(jnp.bfloat16), shaped_v, preferred_element_type=jnp.float32
    )
    return (
        row_top.reshape(rows_here, heads_here),
        totals.reshape(rows_here, heads_here),
        numerator.reshape(rows_here, heads_here * HD),
    )


def run_experts(arrived, gate_weight, up_weight, down_weight):
    gate_part = jnp.einsum(
        "secd,edf->secf", arrived, gate_weight, preferred_element_type=jnp.float32
    )
    up_part = jnp.einsum("secd,edf->secf", arrived, up_weight, preferred_element_type=jnp.float32)
    hidden = (jax.nn.silu(gate_part) * up_part).astype(jnp.bfloat16)
    return jnp.einsum(
        "secf,efd->secd", hidden, down_weight, preferred_element_type=jnp.float32
    ).astype(jnp.bfloat16)


def on_device(
    queries,
    cache_keys,
    cache_values,
    span_starts,
    out_weight,
    norm_gain,
    expert_ids,
    gate_fixed,
    gate_weight,
    up_weight,
    down_weight,
):
    gathered = lax.all_gather(queries, "blk", axis=0, tiled=True)
    total_rows = gathered.shape[0]
    width = gathered.shape[1]
    span_length = total_rows // SPANS
    token_index = jnp.arange(total_rows, dtype=jnp.int32)
    span_index = token_index // span_length
    span_match = span_index[:, None] == jnp.arange(SPANS, dtype=jnp.int32)[None, :]
    start_of = jnp.sum(jnp.where(span_match, span_starts[None, :], 0), axis=1)
    query_pos = start_of + token_index % span_length
    cache_rows = cache_keys.shape[0]
    key_pos = lax.axis_index("blk") * cache_rows + jnp.arange(cache_rows, dtype=jnp.int32)
    block_rows = math.gcd(total_rows, 128)
    block_count = total_rows // block_rows

    def one_block(item):
        return partial_attention(item[0], item[1], cache_keys, cache_values, key_pos)

    blocked = (
        gathered.reshape(block_count, block_rows, width),
        query_pos.reshape(block_count, block_rows),
    )
    row_top, totals, numerator = lax.map(one_block, blocked)
    heads_here = row_top.shape[2]
    row_top = row_top.reshape(total_rows, heads_here)
    totals = totals.reshape(total_rows, heads_here)
    numerator = numerator.reshape(total_rows, heads_here * HD)
    global_top = lax.pmax(row_top, "blk")
    factor = jnp.exp(row_top - global_top)
    totals = totals * factor
    numerator = (numerator.reshape(total_rows, heads_here, HD) * factor[:, :, None]).reshape(
        total_rows, heads_here * HD
    )
    own_numer = lax.psum_scatter(
        numerator.astype(jnp.bfloat16), "blk", scatter_dimension=1, tiled=True
    ).astype(jnp.float32)
    all_totals = lax.psum(totals, "blk")
    col_width = own_numer.shape[1]
    first_col = lax.axis_index("blk") * col_width
    spread = jnp.repeat(all_totals, HD, axis=1)
    col_totals = lax.dynamic_slice_in_dim(spread, first_col, col_width, 1)
    attended = (own_numer / col_totals).astype(jnp.bfloat16)
    projected = lax.psum_scatter(
        jnp.dot(attended, out_weight, preferred_element_type=jnp.float32),
        ("blk", "rows"),
        scatter_dimension=0,
        tiled=True,
    )
    attn_proj = projected.astype(jnp.bfloat16)
    values_f = attn_proj.astype(jnp.float32)
    mean_square = jnp.mean(values_f * values_f, axis=-1, keepdims=True)
    normed = (values_f * lax.rsqrt(mean_square + EPSILON) * norm_gain.astype(jnp.float32)).astype(
        jnp.bfloat16
    )
    own_tokens = normed.shape[0]
    top_count = expert_ids.shape[1]
    owners = lax.axis_size("blk") * lax.axis_size("rows")
    local_experts = gate_weight.shape[0]
    expert_count = owners * local_experts
    capacity = min(own_tokens, max(2, 2 * top_count * own_tokens // expert_count))
    slot_total = expert_count * capacity
    route_expert = expert_ids.reshape(-1)
    route_count = route_expert.shape[0]
    hits = (route_expert[:, None] == jnp.arange(expert_count, dtype=jnp.int32)[None, :]).astype(
        jnp.int32
    )
    slot_number = jnp.sum(jnp.cumsum(hits, axis=0) * hits, axis=1) - 1
    target = route_expert * capacity + slot_number
    placed = target[:, None] == jnp.arange(slot_total, dtype=jnp.int32)[None, :]
    route_token = jnp.arange(route_count, dtype=jnp.int32) // top_count
    token_pick = route_token[:, None] == jnp.arange(own_tokens, dtype=jnp.int32)[None, :]
    slot_token = jnp.dot(
        placed.astype(jnp.bfloat16).T,
        token_pick.astype(jnp.bfloat16),
        preferred_element_type=jnp.float32,
    ).astype(jnp.bfloat16)
    outgoing = jnp.dot(slot_token, normed, preferred_element_type=jnp.float32).astype(jnp.bfloat16)
    outgoing = outgoing.reshape(owners, local_experts, capacity, -1)
    gate_values = gate_fixed.astype(jnp.float32)
    route_weight = (gate_values / jnp.sum(gate_values, axis=1, keepdims=True)).reshape(-1)
    weighted_pick = token_pick.astype(jnp.float32) * route_weight[:, None]
    blend = jnp.dot(weighted_pick.T, placed.astype(jnp.float32), precision=lax.Precision.HIGHEST)
    finished = run_experts(
        lax.all_to_all(outgoing, ("blk", "rows"), split_axis=0, concat_axis=0, tiled=True),
        gate_weight,
        up_weight,
        down_weight,
    )
    returned = lax.all_to_all(finished, ("blk", "rows"), split_axis=0, concat_axis=0, tiled=True)
    returned_flat = returned.reshape(slot_total, -1)
    mixed = jnp.dot(blend, returned_flat.astype(jnp.float32), precision=lax.Precision.HIGHEST)
    expert_out = mixed.astype(jnp.bfloat16)
    return (attn_proj, expert_out)


def solution(mesh):
    in_specs = (
        P(("groups", "blk"), "rows"),
        P(("groups", "blk"), "rows"),
        P(("groups", "blk"), "rows"),
        P("groups"),
        P(("rows", "blk"), None),
        P(),
        P(("groups", "blk", "rows"), None),
        P(("groups", "blk", "rows"), None),
        P(("blk", "rows"), None, None),
        P(("blk", "rows"), None, None),
        P(("blk", "rows"), None, None),
    )
    out_specs = (P(("groups", "blk", "rows"), None), P(("groups", "blk", "rows"), None))
    return jax.shard_map(
        on_device, mesh=mesh, in_specs=in_specs, out_specs=out_specs, check_vma=False
    )
```

profile of v0, /device:TPU:0, one launch (start us, length us, event | category | flops | bytes accessed | tf_op | source)
XLA Modules:
  0.0 247.3 jit_solution(16907521409882701303)
XLA Ops:
  7.3 0.9 fusion.69
  8.2 34.7 %all_gather.3 = bf16[128,1024]{1,0:T(8,128)(2,1)} all-gather(bf16[16,1024]{1,0:T(8,128)(2,1)} %param.11), channel_id=1, replica_groups=mesh['groups'=2,'blk'=8,'rows'=2] {'blk'}, dimensions={0}, use_global_device_ids=true | all-gather | bytes 294912 | tf_op jit(solution)/shard_map/all_gather | solution.py:66
  42.9 1.1 copy.25
  44.0 0.1 broadcast_compare_fusion
  44.2 2.7 %fusion.13 = (f32[128,8]{0,1:T(8,128)S(1)}, f32[512,128,8]{1,0,2:T(8,128)}) fusion(pred[128,512]{0,1:T(8,128)(4,1)S(1)} %broadcast_compare_fusion, bf16[128,8,128]{0,2,1:T(8,128)(2,1)S(1)} %bitcast.116, bf16[512,128]{1,0:T(8,128)(2,1)} %param.12), kind=kOutput, calls=%fused_computation.13 | convolution fusion | flops 135789568 | bytes 2560000 | tf_op jit(solution)/shard_map/while/body/eval_jaxpr/qgjd,kgd->qgjk/dot_general | solution.py:24
  46.8 21.3 %pmax.7 = f32[128,8]{0,1:T(8,128)S(1)} all-reduce(f32[128,8]{0,1:T(8,128)S(1)} %get-tuple-element.24), channel_id=1, replica_groups=mesh['groups'=2,'blk'=8,'rows'=2] {'blk'}, use_global_device_ids=true, to_apply=%region_2.3 | all-reduce | flops 1024 | bytes 8192 | tf_op jit(solution)/shard_map/pmax | solution.py:92
  68.2 2.2 fusion.14
  70.4 1.5 fusion.32
  72.0 0.7 fusion.37
  72.8 17.2 %psum.7 = f32[128,8]{0,1:T(8,128)S(1)} all-reduce(f32[128,8]{0,1:T(8,128)S(1)} %get-tuple-element.22), channel_id=1, replica_groups=mesh['groups'=2,'blk'=8,'rows'=2] {'blk'}, use_global_device_ids=true, to_apply=%region_5.6 | all-reduce | flops 1024 | bytes 8192 | tf_op jit(solution)/shard_map/psum | solution.py:101
  90.0 41.8 %reduce-scatter.3.cloned.1.call-done = bf16[128,128]{0,1:T(8,128)(2,1)} async-done(((bf16[128,1024]{0,1:T(8,128)(2,1)}), bf16[128,128]{0,1:T(8,128)(2,1)}) %reduce-scatter.3.cloned.1.call-update) | async-done | bytes 32784 | tf_op jit(solution)/shard_map/reduce_scatter | solution.py:98
  131.9 2.4 fusion.54
  134.6 0.2 select_reduce_fusion
  134.8 57.2 %reduce-scatter.5.cloned.1.call-done = f32[8,2048]{1,0:T(8,128)} async-done(((f32[128,2048]{1,0:T(8,128)}), f32[8,2048]{1,0:T(8,128)}) %reduce-scatter.5.cloned.1.call-update) | async-done | bytes 65552 | tf_op jit(solution)/shard_map/reduce_scatter | solution.py:107
  191.9 1.0 fusion.51
  192.9 1.4 fusion.12
  194.3 18.1 %all_to_all.10 = bf16[16,1,8,2048]{3,2,1,0:T(8,128)(2,1)S(1)} all-to-all(bf16[16,1,8,2048]{3,2,1,0:T(8,128)(2,1)} %fusion.12), channel_id=1, replica_groups=mesh['groups'=2,'blk'=8,'rows'=2] {'blk','rows'}, dimensions={0} | all-to-all | bytes 1048576 | tf_op jit(solution)/shard_map/all_to_all | solution.py:148
  212.4 0.8 copy-done.2
  213.2 2.5 fusion.16
  215.7 4.1 %fusion.9 = bf16[16,1,8,2048]{3,2,1,0:T(8,128)(2,1)} fusion(bf16[1,768,2048]{2,1,0:T(8,128)(2,1)S(1)} %copy-done, bf16[1,2048,768]{2,1,0:T(8,128)(2,1)} %param.20, bf16[16,1,8,2048]{3,2,1,0:T(8,128)(2,1)} %copy-done.2, f32[16,1,8,768]{3,2,0,1:T(8,128)S(1)} %fusion.16), kind=kOutput, calls=%fused_computation.8 | convolution fusion | flops 806158336 | bytes 7733248 | tf_op jit(solution)/shard_map/secf,efd->secd/dot_general | solution.py:48
  219.8 4.2 %all-to-all-start.1 = ((bf16[16,1,8,2048]{3,2,1,0:T(8,128)(2,1)}), bf16[16,1,8,2048]{3,2,1,0:T(8,128)(2,1)}, u32[]{:S(2)}, u32[]{:S(2)}) async-start(bf16[16,1,8,2048]{3,2,1,0:T(8,128)(2,1)} %fusion.9), calls=%async_computation.3 | async-start | bytes 1048576 | tf_op jit(solution)/shard_map/all_to_all | solution.py:153
  224.3 0.3 fusion.58
  224.6 13.9 %all-to-all-done.1 = bf16[16,1,8,2048]{3,2,1,0:T(8,128)(2,1)} async-done(((bf16[16,1,8,2048]{3,2,1,0:T(8,128)(2,1)}), bf16[16,1,8,2048]{3,2,1,0:T(8,128)(2,1)}, u32[]{:S(2)}, u32[]{:S(2)}) %all-to-all-start.1) | async-done | bytes 524320 | tf_op jit(solution)/shard_map/all_to_all | solution.py:153
  238.5 2.0 convolution_convert_fusion.1
  (31 shorter events, 0.7 us)
Async XLA Ops:
  7.2 208.6 %copy-start = (bf16[1,768,2048]{2,1,0:T(8,128)(2,1)S(1)}, bf16[1,768,2048]{2,1,0:T(8,128)(2,1)}, u32[]{:S(2)}) copy-start(bf16[1,768,2048]{2,1,0:T(8,128)(2,1)} %param.21) | copy-start | bytes 9437188
  7.2 124.7 %reduce-scatter.3.cloned.1.call-start = ((), (), s32[]{:S(2)}) async-start(), calls=%async_computation.4 | async-start | bytes 294912 | tf_op jit(solution)/shard_map/reduce_scatter | solution.py:98
  68.2 2.3 copy-start.1
  72.0 62.3 %copy-start.6 = (s32[8,8]{1,0:T(8,128)S(1)}, s32[8,8]{1,0:T(8,128)}, u32[]{:S(2)}) copy-start(s32[8,8]{1,0:T(8,128)} %param.17) | copy-start | bytes 772
  72.0 62.5 %copy-start.5 = (bf16[2048]{0:T(1024)(128)(2,1)S(1)}, bf16[2048]{0:T(1024)(128)(2,1)}, u32[]{:S(2)}) copy-start(bf16[2048]{0:T(1024)(128)(2,1)} %param.16) | copy-start | bytes 12292
  72.8 119.1 %reduce-scatter.5.cloned.1.call-start = ((), (), s32[]{:S(2)}) async-start(), calls=%async_computation.5 | async-start | bytes 1114112 | tf_op jit(solution)/shard_map/reduce_scatter | solution.py:107
  192.9 1.4 copy-start.3
  212.4 0.8 copy-start.2
  215.7 8.3 %copy-start.4 = (s32[8,8]{1,0:T(8,128)S(1)}, s32[8,8]{1,0:T(8,128)}, u32[]{:S(2)}) copy-start(s32[8,8]{1,0:T(8,128)} %param.18) | copy-start | bytes 772
  219.8 18.7 %all-to-all-start.1 = ((bf16[16,1,8,2048]{3,2,1,0:T(8,128)(2,1)}), bf16[16,1,8,2048]{3,2,1,0:T(8,128)(2,1)}, u32[]{:S(2)}, u32[]{:S(2)}) async-start(bf16[16,1,8,2048]{3,2,1,0:T(8,128)(2,1)} %fusion.9), calls=%async_computation.3 | async-start | bytes 1048576 | tf_op jit(solution)/shard_map/all_to_all | solution.py:153
Sparse Core Ops, SparseCore 0:
  72.9 58.8 reduce-scatter.2
  135.5 56.4 reduce-scatter.4
where the time goes:
time: 248 us; the launch traced here: 247 us
  waiting for transfers between devices  113 us (46%)
  blocking collectives  91.4 us (37%)
  matrix products  16.8 us (7%)
  between operations  14.2 us (6%)
  other arithmetic  5.54 us (2%)
  starting transfers between devices  4.32 us (2%)
    reduce_scatter x1, waiting for transfers between devices, on_device(): lax.psum_scatter(jnp.dot(attended, out_weight, preferred_element_type=jnp...  57.2 us
    reduce_scatter x1, waiting for transfers between devices, on_device(): lax.psum_scatter(numerator.astype(jnp.bfloat16), 'blk', scatter_dimension...  41.8 us
    all_gather x1, blocking collectives, on_device(): gathered = lax.all_gather(queries, 'blk', axis=0, tiled=True)  34.7 us
    pmax x1, blocking collectives, on_device(): global_top = lax.pmax(row_top, 'blk')  21.3 us
    all_to_all x1, blocking collectives, on_device(): lax.all_to_all(outgoing, ('blk', 'rows'), split_axis=0, concat_axis=0, ti...  18.1 us
    psum x1, blocking collectives, on_device(): all_totals = lax.psum(totals, 'blk')  17.2 us
    all_to_all x1, waiting for transfers between devices, on_device(): lax.all_to_all(finished, ('blk', 'rows'), split_axis=0, concat_axis=0, ti...  13.9 us
  transfers between devices with their start and end apart: 3, of which 3 were waited for; matrix products, arithmetic and copies ran while one was open for 0% of the time, Pallas kernels for 0%

commit v1 on v0

v1 whole, which is shorter than its diff:
```python
import functools
import math

import jax
import jax.numpy as jnp
from jax import lax
from jax.experimental import pallas as pl
from jax.experimental.pallas import tpu as pltpu
from jax.sharding import PartitionSpec as P

HD = 128
NEG_FILL = -1e30
EPSILON = 1e-06
LANES = 128
PARTS = 2
MESH = pl.DeviceIdType.MESH
F32 = jnp.float32
BF16 = jnp.bfloat16


def fused(
    n,
    q_hbm,
    k_hbm,
    v_hbm,
    starts,
    ow_hbm,
    gain_ref,
    ids_ref,
    gates_ref,
    g_hbm,
    u_hbm,
    d_hbm,
    proj_ref,
    out_ref,
    qbuf,
    kbuf,
    vbuf,
    owbuf,
    gbuf,
    ubuf,
    dbuf,
    wbuf,
    num_send,
    num_recv,
    st_send,
    st_recv,
    att_rows,
    sib_send,
    sib_recv,
    acc,
    red_send,
    red_recv,
    xbuf,
    xs,
    local_sem,
    q_sems,
    w_sems,
    num_sems,
    st_sems,
    red_sems,
    x_sems,
    fwd_sems,
    sib_sems,
    wf_sems,
):
    b = lax.axis_index("blk")
    r = lax.axis_index("rows")
    other = 1 - r
    own_q, width = q_hbm.shape
    rows_t = n * own_q
    tokens = own_q // 2
    heads = width // HD
    cw = width // n
    per_head = HD // cw
    keys = k_hbm.shape[0]
    d_model = ow_hbm.shape[1]
    half = d_model // 2
    part = half // PARTS
    spans = starts.shape[0]

    def peer(j):
        return lax.rem(b + j, n)

    loads = [
        pltpu.make_async_copy(src, dst, local_sem.at[i])
        for i, (src, dst) in enumerate(
            (
                (q_hbm, qbuf.at[b]),
                (k_hbm, kbuf),
                (v_hbm, vbuf),
                (ow_hbm, owbuf),
                (g_hbm.at[0], gbuf),
                (u_hbm.at[0], ubuf),
                (d_hbm.at[0], dbuf),
            )
        )
    ]
    for load in loads:
        load.start()

    barrier = pltpu.get_barrier_semaphore()

    def greet(j, carry):
        pl.semaphore_signal(barrier, inc=1, device_id={"blk": peer(j)}, device_id_type=MESH)
        return carry

    lax.fori_loop(1, n, greet, 0)
    pl.semaphore_signal(barrier, inc=1, device_id={"rows": other}, device_id_type=MESH)

    gates = gates_ref[...].astype(F32)
    share = gates / jnp.sum(gates, axis=1, keepdims=True)
    ids = ids_ref[...]
    lane = lax.broadcasted_iota(jnp.int32, wbuf.shape[2:], 1)
    table = jnp.zeros(wbuf.shape[2:], F32)
    for k in range(ids_ref.shape[1]):
        table = table + jnp.where(ids[:, k : k + 1] == lane, share[:, k : k + 1], 0.0)
    wbuf[r, b] = table

    pl.semaphore_wait(barrier, n)

    def to_peer(src, dst, sems, p, slot):
        return pltpu.make_async_remote_copy(
            src_ref=src,
            dst_ref=dst,
            send_sem=sems.at[0, p],
            recv_sem=sems.at[1, slot],
            device_id={"blk": p},
            device_id_type=MESH,
        )

    def to_sibling(src, dst, send_sem, recv_sem):
        return pltpu.make_async_remote_copy(
            src_ref=src,
            dst_ref=dst,
            send_sem=send_sem,
            recv_sem=recv_sem,
            device_id={"rows": other},
            device_id_type=MESH,
        )

    def q_copy(p, slot):
        return to_peer(q_hbm, qbuf.at[slot], q_sems, p, slot)

    def w_copy(p, slot):
        return to_peer(wbuf.at[r, slot], wbuf.at[r, slot], w_sems, p, slot)

    def send_queries(j, carry):
        q_copy(peer(j), b).start()
        return carry

    def send_table(j, carry):
        w_copy(peer(j), b).start()
        return carry

    lax.fori_loop(1, n, send_queries, 0)
    lax.fori_loop(1, n, send_table, 0)

    loads[0].wait()
    loads[1].wait()
    loads[2].wait()
    key_block = kbuf[...]
    value_t = vbuf[...].T

    token = lax.broadcasted_iota(jnp.int32, (1, rows_t), 1)
    span_len = rows_t // spans
    start_of = jnp.zeros((1, rows_t), jnp.int32)
    for s in range(spans):
        start_of = jnp.where(token // span_len == s, starts[s], start_of)
    query_pos = start_of + lax.rem(token, span_len)
    limit = query_pos - b * keys
    visible = lax.broadcasted_iota(jnp.int32, (keys, rows_t), 0) <= limit

    def wait_queries(j, carry):
        q_copy(b, peer(j)).wait_recv()
        return carry

    lax.fori_loop(1, n, wait_queries, 0)

    def num_copy(p, slot):
        return to_peer(num_send.at[p], num_recv.at[slot], num_sems, p, slot)

    def st_copy(h, p, slot):
        return to_peer(st_send.at[h], st_recv.at[slot], st_sems, p, slot)

    scale = 1.0 / math.sqrt(HD)
    for j in range(heads):
        h = lax.rem(b // per_head + 1 + j, heads)
        q_h = qbuf[:, :, pl.ds(pl.multiple_of(h * HD, HD), HD)].reshape(rows_t, HD)
        scores = (
            lax.dot_general(key_block, q_h, (((1,), (1,)), ((), ())), preferred_element_type=F32)
            * scale
        )
        scores = jnp.where(visible, scores, NEG_FILL)
        top = jnp.max(scores, axis=0, keepdims=True)
        weights = jnp.where(visible, jnp.exp(scores - top), 0.0)
        total = jnp.sum(weights, axis=0, keepdims=True)
        numer = jnp.dot(value_t, weights.astype(BF16), preferred_element_type=F32)
        st_send[h, 0:1, :] = top
        st_send[h, 1:2, :] = total
        for c in range(per_head):
            num_send[h * per_head + c] = numer[c * cw : (c + 1) * cw].astype(BF16)
        for c in range(per_head):
            p = h * per_head + c

            @pl.when(p != b)
            def _():
                num_copy(p, b).start()
                st_copy(h, p, b).start()

    own_head = b // per_head

    def wait_table(j, carry):
        w_copy(b, peer(j)).wait_recv()
        return carry

    lax.fori_loop(1, n, wait_table, 0)
    table_forward = to_sibling(wbuf.at[r], wbuf.at[r], wf_sems.at[0], wf_sems.at[1])
    table_forward.start()

    num_recv[b] = num_send[b]
    st_recv[b] = st_send[own_head]

    def wait_partial(j, carry):
        num_copy(b, peer(j)).wait_recv()
        st_copy(own_head, b, peer(j)).wait_recv()
        return carry

    lax.fori_loop(1, n, wait_partial, 0)

    tops = st_recv[:, 0:1, :]
    sums = st_recv[:, 1:2, :]
    row_top = jnp.max(tops, axis=0, keepdims=True)
    factors = jnp.exp(tops - row_top)
    inverse = 1.0 / jnp.sum(factors * sums, axis=0)
    mixed = jnp.zeros((cw, rows_t), F32)
    for s in range(n):
        mixed = mixed + num_recv[s].astype(F32) * factors[s]
    attended = (mixed * inverse).T
    att_rows[...] = attended.reshape(n, 2, tokens, cw)

    loads[3].wait()
    half_rows = n * tokens
    att_other = att_rows[:, other].reshape(half_rows, cw).astype(BF16)
    att_mine = att_rows[:, r].reshape(half_rows, cw).astype(BF16)
    att_both = jnp.concatenate([att_other, att_mine], axis=0)

    def stacked(left, right):
        return jnp.concatenate(
            [left.reshape(n, tokens, part), right.reshape(n, tokens, part)], axis=1
        )

    def reduce_scatter(which, columns_of):
        copies = []
        for c in range(PARTS):
            left = columns_of(c * part)
            right = columns_of(half + c * part)
            sib_send[which, c] = stacked(left[:half_rows], right[:half_rows]).astype(BF16)
            copy = to_sibling(
                sib_send.at[which, c],
                sib_recv.at[which, c],
                sib_sems.at[which, 0, c],
                sib_sems.at[which, 1, c],
            )
            copy.start()
            copies.append(copy)
            acc[:, :, c * part : (c + 1) * part] = stacked(left[half_rows:], right[half_rows:])
        for copy in copies:
            copy.wait_recv()

        def summed(p):
            arrived = jnp.concatenate([sib_recv[which, c, p] for c in range(PARTS)], axis=1)
            return acc[p] + arrived.astype(F32)

        sems = red_sems.at[which]

        def red_copy(p, slot):
            return to_peer(red_send.at[which, p], red_recv.at[which, slot], sems, p, slot)

        def send(j, carry):
            p = peer(j)
            red_send[which, p] = summed(p).astype(BF16)
            red_copy(p, b).start()
            return carry

        lax.fori_loop(1, n, send, 0)

        def receive(j, running):
            p = peer(j)
            red_copy(b, p).wait_recv()
            return running + red_recv[which, p].astype(F32)

        result = lax.fori_loop(1, n, receive, summed(b))

        def finish():
            for copy in copies:
                copy.wait_send()

            def done(j, carry):
                red_copy(peer(j), b).wait_send()
                return carry

            lax.fori_loop(1, n, done, 0)

        return result, finish

    projected, finish_proj = reduce_scatter(
        0,
        lambda start: jnp.dot(
            att_both, owbuf[:, start : start + part], preferred_element_type=F32
        ),
    )

    def unstacked(values):
        return jnp.concatenate([values[:tokens], values[tokens:]], axis=1)

    attn_proj = unstacked(projected).astype(BF16)
    proj_ref[...] = attn_proj
    values_f = attn_proj.astype(F32)
    mean_square = jnp.mean(values_f * values_f, axis=-1, keepdims=True)
    gain = gain_ref[...].astype(F32).reshape(1, d_model)
    normed = values_f * lax.rsqrt(mean_square + EPSILON) * gain
    xbuf[r, b] = jnp.concatenate([normed[:, :half], normed[:, half:]], axis=0).astype(BF16)

    def x_copy(p, slot):
        return to_peer(xbuf.at[r, slot], xbuf.at[r, slot], x_sems, p, slot)

    def x_forward(side, slot):
        return to_sibling(
            xbuf.at[side, slot], xbuf.at[side, slot], fwd_sems.at[0, slot], fwd_sems.at[1, slot]
        )

    def send_x(j, carry):
        x_copy(peer(j), b).start()
        return carry

    lax.fori_loop(1, n, send_x, 0)
    x_forward(r, b).start()

    def pass_on(j, carry):
        p = peer(j)
        x_copy(b, p).wait_recv()
        x_forward(r, p).start()
        return carry

    lax.fori_loop(1, n, pass_on, 0)

    table_forward.wait_recv()
    expert = 2 * b + r
    lanes = lax.broadcasted_iota(jnp.int32, (half_rows, wbuf.shape[3]), 1)

    def weight_column(side):
        rows = wbuf[side].reshape(half_rows, wbuf.shape[3])
        return jnp.sum(jnp.where(lanes == expert, rows, 0.0), axis=1, keepdims=True)

    mix = jnp.concatenate([weight_column(other), weight_column(r)], axis=0)

    def lay_out(side, first):
        rows = xbuf[side].astype(F32).reshape(n, 2, tokens, half)
        xs[first : first + half_rows, :half] = rows[:, 0].reshape(half_rows, half).astype(BF16)
        xs[first : first + half_rows, half:] = rows[:, 1].reshape(half_rows, half).astype(BF16)

    lay_out(r, half_rows)
    loads[4].wait()
    loads[5].wait()

    def wait_forwarded(p, carry):
        x_forward(other, p).wait_recv()
        return carry

    lax.fori_loop(0, n, wait_forwarded, 0)
    lay_out(other, 0)

    everyone = xs[...]
    gate_part = jnp.dot(everyone, gbuf[...], preferred_element_type=F32)
    up_part = jnp.dot(everyone, ubuf[...], preferred_element_type=F32)
    hidden = (gate_part / (1.0 + jnp.exp(-gate_part)) * up_part).astype(BF16)
    loads[6].wait()

    def down_columns(start):
        result = jnp.dot(hidden, dbuf[:, start : start + part], preferred_element_type=F32)
        return result.astype(BF16).astype(F32) * mix

    blended, finish_down = reduce_scatter(1, down_columns)
    out_ref[...] = unstacked(blended).astype(BF16)

    def sent(j, carry):
        p = peer(j)
        q_copy(p, b).wait_send()
        w_copy(p, b).wait_send()
        num_copy(p, b).wait_send()
        st_copy(p // per_head, p, b).wait_send()
        x_copy(p, b).wait_send()
        return carry

    lax.fori_loop(1, n, sent, 0)

    def forwarded(p, carry):
        x_forward(r, p).wait_send()
        return carry

    lax.fori_loop(0, n, forwarded, 0)
    table_forward.wait_send()
    finish_proj()
    finish_down()


def solution(mesh):
    n = mesh.shape["blk"]

    def on_device(
        queries,
        cache_keys,
        cache_values,
        span_starts,
        out_weight,
        norm_gain,
        expert_ids,
        gate_fixed,
        gate_weight,
        up_weight,
        down_weight,
    ):
        own_q, width = queries.shape
        tokens, d_model = expert_ids.shape[0], out_weight.shape[1]
        rows_t = n * own_q
        heads = width // HD
        cw = width // n
        half = d_model // 2
        experts = 2 * n * gate_weight.shape[0]
        table_lanes = -(-experts // LANES) * LANES
        dma = pltpu.SemaphoreType.DMA
        anywhere = pl.BlockSpec(memory_space=pl.ANY)
        vmem = pl.BlockSpec(memory_space=pltpu.VMEM)
        smem = pl.BlockSpec(memory_space=pltpu.SMEM)
        out = jax.ShapeDtypeStruct((tokens, d_model), BF16)
        return pl.pallas_call(
            functools.partial(fused, n),
            out_shape=(out, out),
            in_specs=[
                anywhere,
                anywhere,
                anywhere,
                smem,
                anywhere,
                vmem,
                vmem,
                vmem,
                anywhere,
                anywhere,
                anywhere,
            ],
            out_specs=(vmem, vmem),
            scratch_shapes=[
                pltpu.VMEM((n, own_q, width), BF16),
                pltpu.VMEM(cache_keys.shape, BF16),
                pltpu.VMEM(cache_values.shape, BF16),
                pltpu.VMEM(out_weight.shape, BF16),
                pltpu.VMEM(gate_weight.shape[1:], BF16),
                pltpu.VMEM(up_weight.shape[1:], BF16),
                pltpu.VMEM(down_weight.shape[1:], BF16),
                pltpu.VMEM((2, n, tokens, table_lanes), F32),
                pltpu.VMEM((n, cw, rows_t), BF16),
                pltpu.VMEM((n, cw, rows_t), BF16),
                pltpu.VMEM((heads, 8, rows_t), F32),
                pltpu.VMEM((n, 8, rows_t), F32),
                pltpu.VMEM((n, 2, tokens, cw), F32),
                pltpu.VMEM((2, PARTS, n, 2 * tokens, half // PARTS), BF16),
                pltpu.VMEM((2, PARTS, n, 2 * tokens, half // PARTS), BF16),
                pltpu.VMEM((n, 2 * tokens, half), F32),
                pltpu.VMEM((2, n, 2 * tokens, half), BF16),
                pltpu.VMEM((2, n, 2 * tokens, half), BF16),
                pltpu.VMEM((2, n, 2 * tokens, half), BF16),
                pltpu.VMEM((rows_t, d_model), BF16),
                dma((7,)),
                dma((2, n)),
                dma((2, n)),
                dma((2, n)),
                dma((2, n)),
                dma((2, 2, n)),
                dma((2, n)),
                dma((2, n)),
                dma((2, 2, PARTS)),
                dma((2,)),
            ],
            compiler_params=pltpu.CompilerParams(
                collective_id=0, has_side_effects=True, vmem_limit_bytes=56 * 1024 * 1024
            ),
        )(
            queries,
            cache_keys,
            cache_values,
            span_starts,
            out_weight,
            norm_gain,
            expert_ids,
            gate_fixed,
            gate_weight,
            up_weight,
            down_weight,
        )

    in_specs = (
        P(("groups", "blk"), "rows"),
        P(("groups", "blk"), "rows"),
        P(("groups", "blk"), "rows"),
        P("groups"),
        P(("rows", "blk"), None),
        P(),
        P(("groups", "blk", "rows"), None),
        P(("groups", "blk", "rows"), None),
        P(("blk", "rows"), None, None),
        P(("blk", "rows"), None, None),
        P(("blk", "rows"), None, None),
    )
    out_specs = (P(("groups", "blk", "rows"), None), P(("groups", "blk", "rows"), None))
    return jax.shard_map(
        on_device, mesh=mesh, in_specs=in_specs, out_specs=out_specs, check_vma=False
    )
```

time: 248 us -> 53.9 us (0.22)
  waiting for transfers between devices: 113 us -> 0 us
  blocking collectives: 91.4 us -> 0 us
  Pallas kernels: 0 us -> 50.2 us
  matrix products: 16.8 us -> 0 us
  between operations: 14.2 us -> 0.64 us
  other arithmetic: 5.54 us -> 0 us
  starting transfers between devices: 4.32 us -> 0 us
    reduce_scatter x2 -> x0, waiting for transfers between devices: 99 us -> none  [the longest x1 57.2 us: on_device(): lax.psum_scatter(jnp.dot(attended, out_weight, preferred_element_type=jnp...]
    pallas_call x0 -> x1, Pallas kernels: none -> 50.2 us  [on_device(): pl.pallas_call(functools.partial(fused, n), out_shape=(out, out), in_spec...]
    all_gather x1 -> x0, blocking collectives: 34.7 us -> none  [on_device(): gathered = lax.all_gather(queries, 'blk', axis=0, tiled=True)]
    pmax x1 -> x0, blocking collectives: 21.3 us -> none  [on_device(): global_top = lax.pmax(row_top, 'blk')]
    all_to_all x1 -> x0, blocking collectives: 18.1 us -> none  [on_device(): lax.all_to_all(outgoing, ('blk', 'rows'), split_axis=0, concat_axis=0, ti...]
    psum x1 -> x0, blocking collectives: 17.2 us -> none  [on_device(): all_totals = lax.psum(totals, 'blk')]
    dot_general x8 -> x0, matrix products: 16.8 us -> none  [the longest x1 4.08 us: run_experts(): jnp.einsum('secf,efd->secd', hidden, down_weight, preferred_element_type=...]
    all_to_all x1 -> x0, waiting for transfers between devices: 13.9 us -> none  [on_device(): lax.all_to_all(finished, ('blk', 'rows'), split_axis=0, concat_axis=0, ti...]
  transfers between devices with their start and end apart: 3 -> 0, of which waited for: 3 -> 0; matrix products, arithmetic and copies ran while one was open for 0% -> 0% of each run, Pallas kernels for 0% -> 0%
where the time goes in v1:
time: 53.9 us; the launch traced here: 53.6 us
  Pallas kernels  50.2 us (93%)
  local copies, waits for them, and re-layouts  2.75 us (5%)
  between operations  0.64 us (1%)
    pallas_call x1, Pallas kernels, on_device(): pl.pallas_call(functools.partial(fused, n), out_shape=(out, out), in_spec...  50.2 us
    unnamed x2, local copies, waits for them, and re-layouts  2.75 us

profile of v1, /device:TPU:0, one launch (start us, length us, event | category | flops | bytes accessed | tf_op | source)
XLA Modules:
  0.0 53.6 jit_solution(8363034581247137821)
XLA Ops:
  0.6 50.2 %shard_map.122 = (bf16[8,2048]{1,0:T(8,128)(2,1)}, bf16[8,2048]{1,0:T(8,128)(2,1)}) custom-call(bf16[16,1024]{1,0:T(8,128)(2,1)} %q_hbm.1, bf16[512,128]{1,0:T(8,128)(2,1)} %k_hbm.1, bf16[512,128]{1,0:T(8,128)(2,1)} %v_hbm.1, s32[2]{0:T(128)} %starts.1, bf16[128,2048]{1,0:T(8,128)(2,1)} %ow_hbm.1, bf16[2048]{0:T(1024)(128)(2,1)} %gain_ref.1, ...), custom_call_target="tpu_custom_call" | custom-call | tf_op jit(solution)/shard_map/pallas_call | solution.py:437
  50.8 1.4 %copy.15 = bf16[8,2048]{1,0:T(8,128)(2,1)} copy(bf16[8,2048]{1,0:T(8,128)(2,1)} %get-tuple-element.4) | data formatting | bytes 65536
  52.2 1.4 %copy.16 = bf16[8,2048]{1,0:T(8,128)(2,1)} copy(bf16[8,2048]{1,0:T(8,128)(2,1)} %get-tuple-element.5) | data formatting | bytes 65536

commit v2 on v1

--- a/solution.py
+++ b/solution.py
@@ -31,8 +31,7 @@
     g_hbm,
     u_hbm,
     d_hbm,
-    proj_ref,
-    out_ref,
+    both_ref,
     qbuf,
     kbuf,
     vbuf,
@@ -315,8 +314,8 @@
         return jnp.concatenate([values[:tokens], values[tokens:]], axis=1)
 
     attn_proj = unstacked(projected).astype(BF16)
-    proj_ref[...] = attn_proj
     values_f = attn_proj.astype(F32)
+    both_ref[:tokens] = values_f
     mean_square = jnp.mean(values_f * values_f, axis=-1, keepdims=True)
     gain = gain_ref[...].astype(F32).reshape(1, d_model)
     normed = values_f * lax.rsqrt(mean_square + EPSILON) * gain
@@ -382,7 +381,7 @@
         return result.astype(BF16).astype(F32) * mix
 
     blended, finish_down = reduce_scatter(1, down_columns)
-    out_ref[...] = unstacked(blended).astype(BF16)
+    both_ref[tokens:] = unstacked(blended)
 
     def sent(j, carry):
         p = peer(j)
@@ -433,10 +432,9 @@
         anywhere = pl.BlockSpec(memory_space=pl.ANY)
         vmem = pl.BlockSpec(memory_space=pltpu.VMEM)
         smem = pl.BlockSpec(memory_space=pltpu.SMEM)
-        out = jax.ShapeDtypeStruct((tokens, d_model), BF16)
-        return pl.pallas_call(
+        both = pl.pallas_call(
             functools.partial(fused, n),
-            out_shape=(out, out),
+            out_shape=jax.ShapeDtypeStruct((2 * tokens, d_model), F32),
             in_specs=[
                 anywhere,
                 anywhere,
@@ -450,7 +448,7 @@
                 anywhere,
                 anywhere,
             ],
-            out_specs=(vmem, vmem),
+            out_specs=vmem,
             scratch_shapes=[
                 pltpu.VMEM((n, own_q, width), BF16),
                 pltpu.VMEM(cache_keys.shape, BF16),
@@ -499,6 +497,7 @@
             up_weight,
             down_weight,
         )
+        return both[:tokens].astype(BF16), both[tokens:].astype(BF16)
 
     in_specs = (
         P(("groups", "blk"), "rows"),

time: 53.9 us -> 52.6 us (0.976)
  local copies, waits for them, and re-layouts: 2.75 us -> 0.63 us
  other arithmetic: 0 us -> 0.91 us
    unnamed x2 -> x0, local copies, waits for them, and re-layouts: 2.75 us -> none
    another operation x0 -> x1, other arithmetic: none -> 0.91 us
    slice x0 -> x1, local copies, waits for them, and re-layouts: none -> 0.63 us  [on_device(): return (both[:tokens].astype(BF16), both[tokens:].astype(BF16))]
where the time goes in v2:
time: 52.6 us; the launch traced here: 52.4 us
  Pallas kernels  50.2 us (95%)
  other arithmetic  0.91 us (2%)
  between operations  0.64 us (1%)
  local copies, waits for them, and re-layouts  0.63 us (1%)
    pallas_call x1, Pallas kernels, on_device(): pl.pallas_call(functools.partial(fused, n), out_shape=jax.ShapeDtypeStruc...  50.2 us

profile of v2, /device:TPU:0, one launch (start us, length us, event | category | flops | bytes accessed | tf_op | source)
XLA Modules:
  0.0 52.4 jit_solution(2318840363510445028)
XLA Ops:
  0.6 50.2 %shard_map.122 = f32[16,2048]{1,0:T(8,128)} custom-call(bf16[16,1024]{1,0:T(8,128)(2,1)} %q_hbm.1, bf16[512,128]{1,0:T(8,128)(2,1)} %k_hbm.1, bf16[512,128]{1,0:T(8,128)(2,1)} %v_hbm.1, s32[2]{0:T(128)} %starts.1, bf16[128,2048]{1,0:T(8,128)(2,1)} %ow_hbm.1, bf16[2048]{0:T(1024)(128)(2,1)} %gain_ref.1, s32[8,8]{1,0:T(8,128)} %ids_ref.1, s32[8,8]{1,0:T(8,128)} %gates_ref.1, ...), custom_call_target="tpu_custom_call" | custom-call | tf_op jit(solution)/shard_map/pallas_call | solution.py:435
  50.9 0.9 %convert.4 = bf16[16,2048]{1,0:T(8,128)(2,1)S(1)} convert(f32[16,2048]{1,0:T(8,128)} %shard_map.122) | non-fusion elementwise | flops 32768 | bytes 196608 | tf_op jit(solution)/shard_map/convert.1
  51.8 0.6 %fusion = (bf16[8,2048]{1,0:T(8,128)(2,1)}, bf16[8,2048]{1,0:T(8,128)(2,1)}) fusion(bf16[16,2048]{1,0:T(8,128)(2,1)S(1)} %convert.4), kind=kLoop, calls=%fused_computation | loop fusion | bytes 131072 | tf_op jit(solution)/shard_map/slice | solution.py:500
